TPU v7x, 32 devices: a whole 2x2x4 slice. The times are simulated.
32 devices in a mesh: gx: 8 (over z, x), gy: 4 (over y, core).
Axes of the slice: x: 2, y: 2, z: 4, core: 2. Of those that a mesh axis runs over, the one named last changes fastest.
Arguments:
- tokens: int32 [65536], P(('gx', 'gy')), may hold values from 0 to 26
- timesteps: int32 [256], P(('gx', 'gy')), may hold values from 0 to 999
- cotangent: bfloat16 [65536, 512], P(('gx', 'gy')), may hold values from -6 to 6
- char_table: bfloat16 [27, 512], P(None, ('gx', 'gy')), may hold values from -6 to 6
- time_weight: bfloat16 [512, 512], P(('gx', 'gy')), may hold values from -0.25 to 0.25
- ln1_gain: bfloat16 [512], P(('gx', 'gy')), may hold values from 0.5 to 1.5
- ln1_bias: bfloat16 [512], P(('gx', 'gy')), may hold values from -4 to 4
- w_qkv: bfloat16 [512, 1536], P(('gx', 'gy')), may hold values from -0.25 to 0.25
- w_attn_out: bfloat16 [512, 512], P(('gx', 'gy')), may hold values from -2 to 2
- ln2_gain: bfloat16 [512], P(('gx', 'gy')), may hold values from 0.5 to 1.5
- ln2_bias: bfloat16 [512], P(('gx', 'gy')), may hold values from -4 to 4
- w_up: bfloat16 [512, 2048], P(('gx', 'gy')), may hold values from -0.25 to 0.25
- w_down: bfloat16 [2048, 512], P(('gx', 'gy')), may hold values from -0.125 to 0.125
Outputs:
- result: float32 [65536, 512], P(('gx', 'gy'))
- d_input: float32 [65536, 512], P(('gx', 'gy'))
- d_char_table: float32 [27, 512], P(None, ('gx', 'gy'))
- d_time_weight: float32 [512, 512], P(('gx', 'gy'))
- d_ln1_gain: float32 [512], P(('gx', 'gy'))
- d_ln1_bias: float32 [512], P(('gx', 'gy'))
- d_w_qkv: float32 [512, 1536], P(('gx', 'gy'))
- d_w_attn_out: float32 [512, 512], P(('gx', 'gy'))
- d_ln2_gain: float32 [512], P(('gx', 'gy'))
- d_ln2_bias: float32 [512], P(('gx', 'gy'))
- d_w_up: float32 [512, 2048], P(('gx', 'gy'))
- d_w_down: float32 [2048, 512], P(('gx', 'gy'))
All inputs are finite; a program needn't handle non-finite values.
Results may differ from a plain program's by a relative error of at most 0.013.
Values may be sent and summed in bfloat16 or wider, within the bound.
A program may use at most 192 MiB of HBM per device.

v0:
```python
import math
import types

import jax
import jax.numpy as jnp
from jax import lax
from jax.experimental import pallas as pl
from jax.experimental.pallas import tpu as pltpu
from jax.sharding import PartitionSpec as P

F32, BF16 = jnp.float32, jnp.bfloat16
MESH = pl.DeviceIdType.MESH
AXES = ("gx", "gy")
HEADS = 8
EPSILON = 1e-05
VMEM_LIMIT = 63 * 2**20
BLOCKS = (2, 2, 2)
X, Y, CORE = range(3)


def place():
    gx, gy = lax.axis_index(AXES[0]), lax.axis_index(AXES[1])
    return gx // 2, gx % 2, gy // 2, gy % 2


def device(z, x, y, c):
    return (z * 2 + x, y * 2 + c)


def across(axis):
    z, x, y, c = place()
    return ((z, 1 - x, y, c), (z, x, 1 - y, c), (z, x, y, 1 - c))[axis]


def greet(nz):
    z, x, y, c = place()
    barrier = pltpu.get_barrier_semaphore()
    for where in [across(axis) for axis in (X, Y, CORE)] + [((z + d) % nz, x, y, c) for d in range(1, nz)]:
        pl.semaphore_signal(barrier, inc=1, device_id=device(*where), device_id_type=MESH)


def greeted(nz):
    pl.semaphore_wait(pltpu.get_barrier_semaphore(), 3 + nz - 1)


def halves(width):
    middle = width // 256 * 128
    return pl.ds(0, middle), pl.ds(middle, width - middle)


def blocks_of(out, number):
    if number % 4:
        return out.at[pl.ds(0, number), 0, 0, 0]
    return out.at[pl.ds(0, number // 4), :, :, 0]


class Gather:
    LINES, SIDES, CORNERS, CORES = range(4)

    @staticmethod
    def scratch(nz):
        return pltpu.SemaphoreType.DMA((2, 4))

    def __init__(self, nz, shard, out, sems):
        self.nz, self.shard, self.out, self.sems = nz, shard, out, sems
        self.zs, self.count, self.base, self.waits = pl.ds(0, nz), nz, 0, True

    def send(self, src, dst, sent, came, where):
        return pltpu.make_async_remote_copy(
            src_ref=src, dst_ref=dst, send_sem=self.sems.at[0, sent + (self.base if sent else 0)],
            recv_sem=self.sems.at[1, came + (self.base if came else 0)], device_id=device(*where), device_id_type=MESH)

    def some(self, number, stage):
        ref = blocks_of(self.out, number)
        return self.send(ref, ref, stage, stage, across(CORE))

    def pass_on(self, axis, a, b, sent, came, cut=None):
        c = place()[3]
        ref = self.out.at[self.zs, a, b, c]
        if cut is not None:
            ref = ref.at[:, :, cut]
        self.send(ref, ref, sent, came, across(axis)).start()

    def lines(self):
        z, x, y, c = place()
        for d in range(1, self.nz):
            self.send(self.shard, self.out.at[z, x, y, c], self.LINES, self.LINES, ((z + d) % self.nz, x, y, c)).start()

    def arrived(self):
        self.some(self.nz - 1, self.LINES).wait_recv()

    def sides(self):
        _, x, y, _ = place()
        if self.waits:
            self.arrived()
        self.pass_on(X, x, y, self.SIDES, self.SIDES)
        self.pass_on(Y, x, y, self.SIDES, self.SIDES)
        self.pass_on(CORE, x, y, self.SIDES, self.CORES)

    def corners(self):
        _, x, y, _ = place()
        lo, hi = halves(self.out.shape[-1])
        self.some(2 * self.count, self.SIDES).wait_recv()
        self.pass_on(X, x, 1 - y, self.CORNERS, self.CORNERS, lo)
        self.pass_on(Y, 1 - x, y, self.CORNERS, self.CORNERS, hi)
        self.pass_on(CORE, 1 - x, y, self.CORNERS, self.CORES)
        self.pass_on(CORE, x, 1 - y, self.CORNERS, self.CORES)

    def cores(self):
        _, x, y, _ = place()
        self.some(self.count, self.CORNERS).wait_recv()
        self.pass_on(CORE, 1 - x, 1 - y, self.CORES, self.CORES)

    def whole(self):
        self.some(4 * self.count, self.CORES).wait_recv()

    def sent(self):
        self.some(3 * self.count, self.SIDES).wait_send()
        self.some(3 * self.count, self.CORNERS).wait_send()
        self.some(self.count, self.CORES).wait_send()

    def finish(self):
        self.some(self.nz - 1, self.LINES).wait_send()
        self.sent()


class GatherLayers(Gather):
    @staticmethod
    def scratch(nz):
        return pltpu.SemaphoreType.DMA((2, 1 + 3 * nz))

    def layer(self, j):
        one = Gather(self.nz, self.shard, self.out, self.sems)
        one.zs, one.count, one.base, one.waits = pl.ds(j, 1), 1, 3 * j, False
        return one

    def sent(self):
        for j in range(self.nz):
            self.layer(j).sent()


class Scatter:
    @staticmethod
    def scratch(nz, tail):
        return [pltpu.VMEM((nz, 2, 2) + tail, BF16), pltpu.VMEM((nz,) + tail, BF16), pltpu.VMEM((2, nz) + tail, BF16),
                pltpu.VMEM((nz - 1,) + tail, BF16), pltpu.SemaphoreType.DMA((2, 4))]

    def __init__(self, nz, mine, temps, kept=None):
        self.nz, self.mine, self.kept = nz, mine, kept
        self.own, self.far, self.near, self.line, self.sems = temps
        self.width = self.own.shape[-1]

    def send(self, src, dst, stage, where):
        return pltpu.make_async_remote_copy(
            src_ref=src, dst_ref=dst, send_sem=self.sems.at[0, stage], recv_sem=self.sems.at[1, stage],
            device_id=device(*where), device_id_type=MESH)

    def done(self, ref, stage):
        self.send(ref, ref, stage, across(CORE)).wait()

    def add(self, a, b, cols, *values):
        spot = (slice(None), a, b, slice(None), cols)
        total = self.own[spot]
        for value in values:
            total = total + value
        self.own[spot] = total

    def cores(self):
        c = place()[3]
        self.send(self.mine.at[pl.ds(0, self.nz), :, :, 1 - c], self.own, 0, across(CORE)).start()

    def corners(self):
        _, x, y, c = place()
        every, all_z = pl.ds(0, self.width), pl.ds(0, self.nz)
        lo, hi = halves(self.width)
        self.done(self.own, 0)
        for number, (a, b) in enumerate(((1 - x, 1 - y), (1 - x, y), (x, 1 - y), (x, y))):
            self.add(a, b, every, self.mine[:, a, b, c] if self.kept is None else self.kept[:, a, b])
            if number == 0:
                self.send(self.own.at[all_z, 1 - x, 1 - y, :, lo], self.far.at[:, :, lo], 1, across(X)).start()
                self.send(self.own.at[all_z, 1 - x, 1 - y, :, hi], self.far.at[:, :, hi], 1, across(Y)).start()

    def sides(self):
        _, x, y, _ = place()
        all_z = pl.ds(0, self.nz)
        lo, hi = halves(self.width)
        self.done(self.far, 1)
        self.add(x, 1 - y, lo, self.far[:, :, lo])
        self.send(self.own.at[all_z, x, 1 - y], self.near.at[1], 2, across(Y)).start()
        self.add(1 - x, y, hi, self.far[:, :, hi])
        self.send(self.own.at[all_z, 1 - x, y], self.near.at[0], 2, across(X)).start()

    def lines(self):
        z, x, y, c = place()
        self.done(self.near, 2)
        self.add(x, y, pl.ds(0, self.width), self.near[0], self.near[1])
        for d in range(1, self.nz):
            to = (z + d) % self.nz
            self.send(self.own.at[to, x, y], self.line.at[d - 1], 3, (to, x, y, c)).start()

    def total(self):
        z, x, y, _ = place()
        self.done(self.line, 3)
        total = self.own[z, x, y].astype(F32)
        for d in range(1, self.nz):
            total = total + self.line[d - 1].astype(F32)
        return total


class Call:
    def __init__(self):
        self.ins, self.outs, self.temps = {}, {}, {}

    def arg(self, **named):
        self.ins.update(named)

    def out(self, **named):
        self.outs.update(named)

    def temp(self, **named):
        self.temps.update(named)

    def run(self, kernel, name, steps=None, collective=None):
        kinds = [k for kind in self.temps.values() for k in (kind if isinstance(kind, list) else [kind])]

        def body(*refs):
            refs = iter(refs)
            r = types.SimpleNamespace(**{n: next(refs) for n in [*self.ins, *self.outs]})
            for n, kind in self.temps.items():
                setattr(r, n, [next(refs) for _ in kind] if isinstance(kind, list) else next(refs))
            kernel(r)
        extra = {} if collective is None else dict(collective_id=collective, has_side_effects=True)
        got = pl.pallas_call(
            body, grid=() if steps is None else (steps,), in_specs=[spec for _, spec in self.ins.values()], out_specs=[spec for *_, spec in self.outs.values()],
            out_shape=[jax.ShapeDtypeStruct(shape, kind) for shape, kind, _ in self.outs.values()], scratch_shapes=kinds,
            compiler_params=pltpu.CompilerParams(vmem_limit_bytes=VMEM_LIMIT, **extra), name=name,
        )(*[array for array, _ in self.ins.values()])
        return types.SimpleNamespace(**dict(zip(self.outs, got)))


def whole(shape):
    return pl.BlockSpec(tuple(shape), lambda i: (0,) * len(shape))


def lanes(rows, width, at=lambda i: i):
    return pl.BlockSpec((rows, width), lambda i: (0, at(i)))


ANYWHERE = pl.BlockSpec(memory_space=pl.ANY)
RESIDENT = pl.BlockSpec(memory_space=pltpu.VMEM)


def at_step(i, table):
    for step, acts in enumerate(table):
        if acts:
            @pl.when(i == step)
            def _():
                for act in acts:
                    act()


def block_at(i, width):
    return pl.ds(pl.multiple_of(i * width, width), width)


def dot(left, right):
    return jnp.dot(left, right, preferred_element_type=F32)


def dot_nt(left, right):
    return lax.dot_general(left, right, (((1,), (1,)), ((), ())), preferred_element_type=F32)


def norm_rows(values):
    count = values.shape[0]
    shifted = values - jnp.sum(values, axis=0, keepdims=True) * (1.0 / count)
    inverse = lax.rsqrt(jnp.sum(shifted * shifted, axis=0, keepdims=True) * (1.0 / count) + EPSILON)
    return shifted * inverse, inverse


def norm_rows_back(grad, gain, normed, inverse):
    count = grad.shape[0]
    scaled = grad * gain
    lean = jnp.sum(scaled, axis=0, keepdims=True) * (1.0 / count)
    turn = jnp.sum(scaled * normed, axis=0, keepdims=True) * (1.0 / count)
    return inverse * (scaled - lean - normed * turn)


def fold(values):
    total = values[:, :128]
    for k in range(1, values.shape[1] // 128):
        total = total + values[:, 128 * k:128 * (k + 1)]
    return total


def flat(ref, cols=slice(None)):
    value = ref[(slice(None),) * (len(ref.shape) - 1) + (cols,)]
    return value.reshape(-1, value.shape[-1])


def param(table, column):
    return table[:, column:column + 1].astype(F32)


def gelu_parts(hidden, grad_active):
    cdf = 0.5 + 0.5 * lax.erf(hidden * math.sqrt(0.5))
    bell = jnp.exp2(hidden * hidden * (-0.5 * math.log2(math.e))) * (1.0 / math.sqrt(2.0 * math.pi))
    return (hidden * cdf).astype(BF16), (grad_active.astype(BF16).astype(F32) * (cdf + hidden * bell)).astype(BF16)


def fill_waves(r, feat):
    half = feat // 2
    r.steps_row[...] = jnp.zeros_like(r.steps_row)
    r.steps_row[:, :r.steps.shape[1]] = r.steps[...].astype(F32)
    rate = jnp.exp(lax.broadcasted_iota(jnp.int32, (half, 128), 0).astype(F32) * (-math.log(10000.0) / half))
    angles = rate * r.steps_row[...]
    r.waves[:half, :] = jnp.sin(angles).astype(BF16)
    r.waves[half:, :] = jnp.cos(angles).astype(BF16)


def fill_small(r, chars):
    count = r.char.shape[0]
    r.square[...] = jnp.zeros_like(r.square)
    for k, ref in enumerate((r.g1, r.b1, r.g2, r.b2)):
        r.square[chars + k:chars + k + 1, :count] = ref[...].astype(F32)
    r.small_shard[...] = r.square[...].T[:count].astype(BF16)
    r.small_shard[:, :chars] = r.char[...]


ITEM_HIGH, ITEM_LOW = 32, 64


def one_hot_of(tok, item):
    row = lax.broadcasted_iota(jnp.int32, (128, tok.shape[1]), 0)
    return ((row == tok) | (row == ITEM_HIGH + item) | (row == ITEM_LOW + item)).astype(BF16)


class Heads:
    def __init__(self, feat):
        self.size = feat // HEADS
        self.q, self.k, self.v = ([pl.ds(part * feat + h * self.size, self.size) for h in range(HEADS)] for part in range(3))

    def scores(self, project, scores):
        for h in range(HEADS):
            scores[h] = dot(project[self.k[h], :].T, project[self.q[h], :])

    def softmax(self, scores, powers, inverses):
        turn = math.log2(math.e) / math.sqrt(self.size)
        for h in range(HEADS):
            value = scores[h]
            power = jnp.exp2((value - jnp.max(value, axis=0, keepdims=True)) * turn)
            inverses[h:h + 1, :] = 1.0 / jnp.sum(power, axis=0, keepdims=True)
            powers[h] = power.astype(BF16)

    def mix(self, project, powers, inverses, mixed):
        for h in range(HEADS):
            mixed[self.q[h], :] = (dot(project[self.v[h], :], powers[h]) * inverses[h:h + 1, :]).astype(BF16)

    def scale_grad(self, grad_mixed, inverses, mixed, scaled, lean):
        for h in range(HEADS):
            value = grad_mixed[self.q[h], :] * inverses[h:h + 1, :]
            lean[h:h + 1, :] = jnp.sum(value * mixed[self.q[h], :].astype(F32), axis=0, keepdims=True)
            scaled[self.q[h], :] = value.astype(BF16)

    def grad_probs(self, project, scaled, scores):
        for h in range(HEADS):
            scores[h] = dot(project[self.v[h], :].T, scaled[self.q[h], :])

    def grad_scores(self, powers, scores, lean, grads):
        for h in range(HEADS):
            grads[h] = (powers[h].astype(F32) * (scores[h] - lean[h:h + 1, :])).astype(BF16)

    def grad_project(self, project, scaled, powers, grads, out, cols):
        scale = 1.0 / math.sqrt(self.size)
        for h in range(HEADS):
            out[self.v[h], cols] = dot_nt(scaled[self.q[h], :], powers[h]).astype(BF16)
            out[self.q[h], cols] = (dot(project[self.k[h], :], grads[h]) * scale).astype(BF16)
            out[self.k[h], cols] = (dot_nt(project[self.q[h], :], grads[h]) * scale).astype(BF16)


class Stream:
    def __init__(self, sems):
        self.sems = sems

    def start(self, number, src, dst):
        pltpu.make_async_copy(src, dst, self.sems.at[number]).start()

    def wait(self, number, src, dst):
        pltpu.make_async_copy(src, dst, self.sems.at[number]).wait()


def forward(nz, tokens, timesteps, cotangent, char, g1, b1, g2, b2, time_w, w_qkv, w_out, w_up, w_down, chunk=512):
    seqs = timesteps.shape[0]
    n = tokens.shape[0]
    length = n // seqs
    feat, ff = time_w.shape[1], w_up.shape[1]
    count, chars = char.shape
    pair = 2 if seqs % 2 == 0 else 1
    items, width = seqs // pair, pair * length
    wide = ff // nz if nz else 512
    tiles, chunks = ff // wide, n // chunk
    share = ff // chunks
    heads = Heads(feat)
    call = Call()
    at_once = lambda value: (value, RESIDENT)
    call.arg(tok=at_once(tokens.reshape(seqs, 1, length)), steps=at_once(timesteps.reshape(1, seqs)), char=at_once(char),
             g1=at_once(g1.reshape(1, count)), b1=at_once(b1.reshape(1, count)), g2=at_once(g2.reshape(1, count)),
             b2=at_once(b2.reshape(1, count)), time_w=at_once(time_w), w_qkv=at_once(w_qkv), w_out=at_once(w_out), w_up=at_once(w_up),
             w_down=at_once(w_down), cot=(cotangent, ANYWHERE))
    call.out(start_o=((feat, n), F32, ANYWHERE), mixed_o=((feat, n), BF16, ANYWHERE), project_o=((3 * feat, n), BF16, ANYWHERE),
             powers_o=((seqs, HEADS, length, length), BF16, ANYWHERE), inv=((seqs, HEADS, length), F32, RESIDENT),
             waves=((feat, 128), BF16, RESIDENT), grad_o=((feat, n), F32, ANYWHERE), ln=((2, feat, 128), F32, RESIDENT),
             d_down_o=((ff, feat), BF16, ANYWHERE), middle_o=((feat, n), F32, ANYWHERE), act_o=((ff, n), BF16, ANYWHERE),
             down_o=((feat, ff), BF16, ANYWHERE))
    parts = 3
    vmem = lambda kind, *shape: pltpu.VMEM(shape, kind)
    if nz:
        per = feat // (nz * 8)
        blocks = lambda *tail: (nz,) + BLOCKS + tail
        landing = lambda *tail: vmem(BF16, *blocks(*tail))
        sems = Gather.scratch(nz)
        call.temp(first=landing(count, 128 + feat), first_sems=sems, out=landing(count, feat), out_sems=sems,
                  qkv=[landing(count, feat)] * parts, qkv_sems=[sems] * parts, ups=vmem(BF16, tiles, *blocks(count, wide)), up_sems=[sems] * tiles,
                  down=landing(*w_down.shape), down_sems=GatherLayers.scratch(nz), first_shard=vmem(BF16, count, 128 + feat),
                  mine=vmem(BF16, tiles, *blocks(per, wide)), sums=Scatter.scratch(nz, (per, wide)) * tiles)
        call.out(first_o=(blocks(count, 128 + feat), BF16, ANYWHERE), out_o=(blocks(count, feat), BF16, ANYWHERE),
                 qkv_o=(blocks(*w_qkv.shape), BF16, ANYWHERE), o_up=((per, ff), F32, RESIDENT))
    else:
        call.out(small=((count, 128), BF16, RESIDENT), d_up=((feat, ff), BF16, RESIDENT))
    call.temp(small_shard=vmem(BF16, count, 128), square=vmem(F32, 128, max(count, 128)), steps_row=vmem(F32, 1, 128),
              table=vmem(BF16, feat, 128), out_t=vmem(BF16, feat, feat), starts=vmem(F32, feat, n), mixed=vmem(BF16, feat, n),
              powers=vmem(BF16, 2, pair, HEADS, length, length), scores=vmem(F32, pair * HEADS, length, length),
              middle=vmem(F32, feat, n), low2=vmem(BF16, feat, n), cot_t=vmem(BF16, max(n, ff), feat), cot_f=vmem(BF16, feat, n),
              down_t=vmem(BF16, feat, ff), up=vmem(BF16, feat, ff), up_t=vmem(BF16, wide, feat),
              act=vmem(BF16, ff, n), gh=vmem(BF16, ff, n), gn=vmem(F32, feat, chunk), tile_down=vmem(BF16, wide, feat),
              sems=pltpu.SemaphoreType.DMA((14 + 2 * chunks,)))

    def kernel(r):
        proj, low = r.act.at[pl.ds(0, 3 * feat)], r.gh.at[pl.ds(0, feat)]
        stream = Stream(r.sems)
        if nz:
            z, x, y, c = place()
            first = Gather(nz, r.first_shard, r.first, r.first_sems)
            qkv = [Gather(nz, r.w_qkv.at[:, pl.ds(p * feat, feat)], r.qkv[p], r.qkv_sems[p]) for p in range(parts)]
            out = Gather(nz, r.w_out, r.out, r.out_sems)
            ups = [Gather(nz, r.w_up.at[:, pl.ds(j * wide, wide)], r.ups.at[j], r.up_sems[j]) for j in range(tiles)]
            down = GatherLayers(nz, r.w_down, r.down, r.down_sems)
            needs = [(ups[j], down.layer(j)) for j in range(tiles)]
            order = [ups[0], ups[1], needs[0][1], needs[1][1]] + [part for some in needs[2:] for part in some]
            groups = [Scatter(nz, r.mine.at[j], r.sums[5 * j:5 * j + 5]) for j in range(tiles)]

        def small():
            return flat(r.first, slice(0, 128)) if nz else r.small[...]

        def stamps(weights):
            stamp = dot(weights.T, r.waves[...])
            lane = lax.broadcasted_iota(jnp.int32, stamp.shape, 1)
            stamp = jnp.where(lane < seqs, stamp, 0.0)
            high = stamp.astype(BF16)
            rest = (stamp - high.astype(F32)).astype(BF16)
            shift = lambda value, by: jnp.concatenate([value[:, 128 - by:], value[:, :128 - by]], axis=1)
            chars_only = jnp.where(lane < chars, small(), jnp.zeros_like(high))
            r.table[...] = chars_only + shift(high, ITEM_HIGH) + shift(rest, ITEM_LOW)

        def begin(some):
            table = small()
            gain, bias = param(table, chars), param(table, chars + 1)
            for k in some:
                cols = pl.ds(k * length, length)
                start = dot(r.table[...], one_hot_of(r.tok[k], k))
                r.starts[:, cols] = start
                normed, _ = norm_rows(start)
                low[:, cols] = (normed * gain + bias).astype(BF16)

        def multiply(p, weights):
            proj[p * feat:(p + 1) * feat] = dot(weights.T, low[...]).astype(BF16)

        to_hbm = [(proj, r.project_o), (r.starts, r.start_o), (r.mixed, r.mixed_o), (r.middle, r.middle_o), (r.act, r.act_o), (r.down_t, r.down_o)]
        if nz:
            every = (pl.ds(0, nz), slice(None), slice(None), slice(None), slice(None))
            to_hbm += [(r.first, r.first_o), (r.out, r.out_o)] + [(g.out, r.qkv_o.at[every + (pl.ds(p * feat, feat),)]) for p, g in enumerate(qkv)]
        cot_in = (11, r.cot, r.cot_t.at[pl.ds(0, n)])

        def leave(*numbers):
            for k in numbers:
                stream.start(k, *to_hbm[k])

        def left(*numbers):
            for k in numbers:
                stream.wait(k, *to_hbm[k])

        def powers_copy(i):
            return 12 + i % 2, r.powers.at[i % 2], r.powers_o.at[pl.ds(i * pair, pair)]

        def grad_copy(m):
            cols = block_at(m, chunk)
            return 14 + m, r.starts.at[:, cols], r.grad_o.at[:, cols]

        def d_down_copy(m):
            rows = block_at(m, share)
            return 14 + chunks + m, r.cot_t.at[rows], r.d_down_o.at[rows]

        def prelude():
            stream.start(*cot_in)
            r.ln[...] = jnp.zeros_like(r.ln)
            if not nz:
                fill_small(r, chars)
                r.small[...] = r.small_shard[...]
                fill_waves(r, feat)
                stamps(r.time_w[...])
                r.out_t[...] = r.w_out[...].T
                begin(range(seqs))
                for p in range(parts):
                    multiply(p, r.w_qkv[:, p * feat:(p + 1) * feat])
                leave(0, 1)
                return
            greet(nz)
            fill_small(r, chars)
            q, k, v = qkv
            r.first_shard[:, :128] = r.small_shard[...]
            r.first_shard[:, 128:] = r.time_w[...]
            for g in (first, out, q, k, v, *ups, down):
                g.out[z, x, y, c] = g.shard[...]
            greeted(nz)
            first.lines()
            q.lines()
            k.lines()
            fill_waves(r, feat)
            first.sides()
            v.lines()
            q.sides()
            out.lines()
            k.sides()
            ups[0].lines()
            first.corners()
            v.sides()
            ups[1].lines()
            q.corners()
            down.lines()
            first.cores()
            k.corners()
            out.sides()
            first.whole()
            stamps(flat(r.first, slice(128, 128 + feat)))
            begin(range(0, seqs // 2))
            q.cores()
            v.corners()
            ups[0].sides()
            begin(range(seqs // 2, seqs))
            k.cores()
            out.corners()
            q.whole()
            multiply(0, flat(r.qkv[0]))
            v.cores()
            ups[1].sides()
            for g in ups[2:]:
                g.lines()
            k.whole()
            multiply(1, flat(r.qkv[1]))
            out.cores()
            down.arrived()
            needs[0][1].sides()
            v.whole()
            multiply(2, flat(r.qkv[2]))
            ups[0].corners()
            out.whole()
            r.out_t[...] = flat(r.out).T
            leave(0, 1, *range(6, 8 + parts))

        def item(i):
            views = []
            for k in range(pair):
                cols = block_at(i * pair + k, length)
                views.append((proj.at[:, cols], r.scores.at[pl.ds(k * HEADS, HEADS)], r.powers.at[i % 2, k], r.inv.at[i * pair + k], r.mixed.at[:, cols]))
            for project, scores, *_ in views:
                heads.scores(project, scores)
            for project, scores, powers, inverses, mixed in views:
                heads.softmax(scores, powers, inverses)
                heads.mix(project, powers, inverses, mixed)
            stream.start(*powers_copy(i))
            cols = block_at(i, width)
            table = small()
            middle = r.starts[:, cols] + dot(r.out_t[...], r.mixed[:, cols])
            r.middle[:, cols] = middle
            normed, _ = norm_rows(middle)
            r.low2[:, cols] = (normed * param(table, chars + 2) + param(table, chars + 3)).astype(BF16)
            r.cot_f[:, cols] = r.cot_t[cols, :].T

        def weights_step(step):
            if not nz:
                return []
            acts = [part.cores for part in order[max(2 * step - 2, 0):2 * step]]
            acts += [part.corners for part in order[max(2 * step, 1):2 * step + 2]]
            return acts + [part.sides for part in order[2 * step + 4 if step else 3:2 * step + 6]]

        def sums_step(step):
            if not nz:
                return []
            return [(g.corners, g.sides, g.lines)[step - j - 1] for j, g in enumerate(groups) if 0 <= step - j - 1 < 3]

        def tile(j):
            rows = block_at(j, wide)
            if nz:
                at_step(j, [[part.whole for part in some] for some in needs])
                r.up[:, rows] = flat(r.ups.at[j])
                r.tile_down[...] = flat(r.down.at[pl.ds(j, 1)])
            else:
                r.up[:, rows] = r.w_up[:, rows]
                r.tile_down[...] = r.w_down[rows, :]
            r.up_t[...] = r.up[:, rows].T
            r.down_t[:, rows] = r.tile_down[...].T
            for t in range(chunks):
                cols = pl.ds(t * chunk, chunk)
                for half in range(2):
                    some = pl.ds(half * wide // 2, wide // 2)
                    part = block_at(2 * j + half, wide // 2)
                    r.act[part, cols], r.gh[part, cols] = gelu_parts(
                        dot(r.up_t[some, :], r.low2[:, cols]), dot(r.tile_down[some, :], r.cot_f[:, cols]))
            at_step(j, [weights_step(items + k) + sums_step(k) for k in range(tiles)])
            d_up = dot_nt(r.low2[...], r.gh[rows, :]).astype(BF16)
            if nz:
                r.mine[j] = d_up.reshape(blocks(per, wide))
                at_step(j, [[g.cores] for g in groups])
            else:
                r.d_up[:, rows] = d_up

        def layer_back(m):
            cols, rows = block_at(m, chunk), block_at(m, share)
            r.gn[...] = dot(r.up[...], r.gh[:, cols])
            r.cot_t[rows, :] = dot_nt(r.act[rows, :], r.cot_f[...]).astype(BF16)
            stream.start(*d_down_copy(m))
            normed, inverse = norm_rows(r.middle[:, cols])
            grad_normed = r.gn[...]
            r.starts[:, cols] = r.cot_f[:, cols].astype(F32) + norm_rows_back(grad_normed, param(small(), chars + 2), normed, inverse)
            r.ln[0] += fold(grad_normed * normed)
            r.ln[1] += fold(grad_normed)
            stream.start(*grad_copy(m))

        prelude()
        stream.wait(*cot_in)

        def items_loop(i, _):
            @pl.when(i >= 2)
            def _():
                stream.wait(*powers_copy(i - 2))
            item(i)
            at_step(i, [weights_step(k) for k in range(items)])
            return 0
        lax.fori_loop(0, items, items_loop, 0)
        left(0, 1)
        leave(2, 3)

        def tiles_loop(j, _):
            tile(j)
            return 0
        lax.fori_loop(0, tiles, tiles_loop, 0)
        leave(4, 5)

        def chunks_loop(m, _):
            layer_back(m)
            at_step(m, [sums_step(tiles + k) for k in range(chunks)])
            return 0
        lax.fori_loop(0, chunks, chunks_loop, 0)
        if nz:
            for g in (first, *qkv, out, *ups, down):
                g.finish()
            for j in range(tiles):
                r.o_up[:, j * wide:(j + 1) * wide] = groups[j].total()
        left(*range(2, len(to_hbm)))
        for i in range(max(items - 2, 0), items):
            stream.wait(*powers_copy(i))
        for m in range(chunks):
            stream.wait(*d_down_copy(m))
            stream.wait(*grad_copy(m))

    return call.run(kernel, "forward_and_ffn", None, 0 if nz else None)


def backward(nz, chars, tokens, small, w_qkv, w_out, saved, chunk=512):
    feat, n = saved.start_o.shape
    seqs = saved.powers_o.shape[0]
    ff = saved.act_o.shape[0]
    length = n // seqs
    pair = 2 if seqs % 2 == 0 else 1
    items, width, chunks = seqs // pair, pair * length, n // chunk
    heads = Heads(feat)
    vmem = lambda kind, *shape: pltpu.VMEM(shape, kind)
    there = lambda value: (value, ANYWHERE)
    call = Call()
    call.arg(tok=(tokens.reshape(seqs, 1, length), RESIDENT), waves=(saved.waves, RESIDENT), inv=(saved.inv, RESIDENT), small_i=there(small),
             qkv_i=there(w_qkv), out_i=there(w_out), start_i=there(saved.start_o), grad_i=there(saved.grad_o), project_i=there(saved.project_o),
             powers_i=there(saved.powers_o), mixed_i=there(saved.mixed_o), ln2_i=there(saved.ln),
             middle_i=there(saved.middle_o), act_i=there(saved.act_o), down_i=there(saved.down_o))
    call.out(d_in=((feat, n), F32, ANYWHERE), result=((feat, n), F32, ANYWHERE))
    call.temp(small=vmem(BF16, feat, 128), qkv=vmem(BF16, feat, 3 * feat), w_out=vmem(BF16, feat, feat), start=vmem(F32, feat, n),
              grad=vmem(F32, feat, n), project=vmem(BF16, 2, 3 * feat, width), powers=vmem(BF16, 2, pair, HEADS, length, length),
              mixed=vmem(BF16, feat, n), ln2=vmem(F32, 2, feat, 128), middle=vmem(F32, feat, n), act=vmem(BF16, 2, ff, chunk),
              down_t=vmem(BF16, feat, ff), ln1=vmem(F32, 2, feat, 128), d_char=vmem(F32, feat, 128), low_f=vmem(BF16, feat, n),
              gp_f=vmem(BF16, 3 * feat, n), ga_f=vmem(BF16, feat, n), scores=vmem(F32, pair * HEADS, length, length),
              grads=vmem(BF16, pair * HEADS, length, length), grad_mixed=vmem(F32, feat, width), scaled=vmem(BF16, feat, width),
              lean=vmem(F32, seqs, HEADS, length), gn=vmem(F32, feat, width), sems=pltpu.SemaphoreType.DMA((12 + 4 * items + chunks,)))
    parts = 4
    if nz:
        devices = nz * 8
        per, down_per = feat // devices, ff // devices
        blocks = (nz,) + BLOCKS
        call.arg(d_down=there(saved.d_down_o.reshape(blocks + (down_per, feat))))
        small_out = lambda *shape: (shape, F32, RESIDENT)
        call.out(o_out=small_out(per, feat), o_down=small_out(down_per, feat), o_qkv=small_out(per, 3 * feat), o_time=small_out(per, feat),
                 o_char=small_out(per, chars), o_ln=small_out(4, per))
        call.temp(down_sums=Scatter.scratch(nz, (down_per, feat)), rest_sums=Scatter.scratch(nz, (per, 128 + feat)),
                  at_sums=Scatter.scratch(nz, (per, feat)) * parts, kept=vmem(BF16, nz, 2, 2, down_per, feat),
                  d_at=[vmem(BF16, *blocks, per, feat)] * parts, d_rest=vmem(BF16, *blocks, per, 128 + feat))
    else:
        call.out(d_at=((feat, 4 * feat), BF16, RESIDENT), d_rest=((feat, 128 + feat), BF16, RESIDENT))

    def kernel(r):
        stream = Stream(r.sems)
        if nz:
            c = place()[3]
            down = Scatter(nz, r.d_down, r.down_sums, r.kept)
            ats = [Scatter(nz, r.d_at[p], r.at_sums[5 * p:5 * p + 5]) for p in range(parts)]
            rest = Scatter(nz, r.d_rest, r.rest_sums)

        def tall(value):
            value = value.astype(BF16)
            return value.reshape(blocks + (per, value.shape[-1])) if nz else value

        def columns(i):
            return block_at(i, width)

        fixed = [(r.out_i, r.w_out), (r.small_i.at[:, pl.ds(0, 128)], r.small), (r.qkv_i, r.qkv), (r.ln2_i, r.ln2), (r.middle_i, r.middle),
                 (r.down_i, r.down_t)]
        if nz:
            fixed.append((r.d_down.at[pl.ds(0, nz), :, :, c], r.kept))

        def fetch(*numbers):
            for k in numbers:
                stream.start(k, *fixed[k])

        def fetched(*numbers):
            for k in numbers:
                stream.wait(k, *fixed[k])

        def item_copies(i):
            cols = columns(i)
            return [(12 + i, r.grad_i.at[:, cols], r.grad.at[:, cols]), (12 + items + i, r.start_i.at[:, cols], r.start.at[:, cols]),
                    (12 + 2 * items + i, r.mixed_i.at[:, cols], r.mixed.at[:, cols]), (8 + i % 2, r.project_i.at[:, cols], r.project.at[i % 2]),
                    (10 + i % 2, r.powers_i.at[pl.ds(i * pair, pair)], r.powers.at[i % 2])]

        def d_in_copy(i):
            return 12 + 3 * items + i, r.start.at[:, columns(i)], r.d_in.at[:, columns(i)]

        def act_copy(m):
            return 8 + m % 2, r.act_i.at[:, block_at(m, chunk)], r.act.at[m % 2]

        def result_copy(m):
            cols = block_at(m, chunk)
            return 12 + 4 * items + m, r.middle.at[:, cols], r.result.at[:, cols]

        def norm_again(i):
            normed, _ = norm_rows(r.start[:, columns(i)])
            r.low_f[:, columns(i)] = (normed * param(r.small[...], chars) + param(r.small[...], chars + 1)).astype(BF16)

        def products():
            pairs = [(r.mixed, r.ga_f)] + [(r.low_f, r.gp_f.at[pl.ds(p * feat, feat)]) for p in range(3)]
            for p, (left, right) in enumerate(pairs):
                product = tall(dot_nt(left[...], right[...]))
                if nz:
                    r.d_at[p][...] = product
                    ats[p].cores()
                    if p > 0:
                        ats[p - 1].corners()
                else:
                    r.d_at[:, p * feat:(p + 1) * feat] = product

        def layer_back(i):
            r.gn[...] = dot(r.qkv[...], r.gp_f[:, columns(i)])
            grad_normed = r.gn[...]
            normed, inverse = norm_rows(r.start[:, columns(i)])
            d_in = r.grad[:, columns(i)] + norm_rows_back(grad_normed, param(r.small[...], chars), normed, inverse)
            r.start[:, columns(i)] = d_in
            stream.start(*d_in_copy(i))
            r.ln1[0] += fold(grad_normed * normed)
            r.ln1[1] += fold(grad_normed)
            one_hot = jnp.concatenate([one_hot_of(r.tok[i * pair + k], i * pair + k) for k in range(pair)], axis=1)
            high = d_in.astype(BF16)
            low = (d_in - high.astype(F32)).astype(BF16)
            r.d_char[...] += dot_nt(high, one_hot) + dot_nt(low, one_hot)

        def rest_products():
            lane = lax.broadcasted_iota(jnp.int32, r.d_char.shape, 1)
            sums = r.d_char[...]
            table = jnp.where(lane < chars, sums, 0.0)
            for k, ref in enumerate((r.ln1.at[0], r.ln1.at[1], r.ln2.at[0], r.ln2.at[1])):
                table = jnp.where(lane == chars + k, jnp.sum(ref[...], axis=1, keepdims=True), table)
            stamps = jnp.concatenate([sums[:, ITEM_HIGH:], sums[:, :ITEM_HIGH]], axis=1)
            stamps = jnp.where(lane < seqs, stamps, 0.0).astype(BF16)
            r.d_rest[..., :128] = tall(table)
            r.d_rest[..., 128:] = tall(dot_nt(r.waves[...], stamps))

        def result(m):
            cols = block_at(m, chunk)
            stream.wait(*act_copy(m))
            r.middle[:, cols] = r.middle[:, cols] + dot(r.down_t[...], r.act[m % 2])
            stream.start(*result_copy(m))

            @pl.when(m + 2 < chunks)
            def _():
                stream.start(*act_copy(m + 2))

        def item(i):
            copies = item_copies(i)
            stream.wait(*copies[0])
            grad_low = r.grad[:, columns(i)].astype(BF16)
            r.ga_f[:, columns(i)] = grad_low
            r.grad_mixed[...] = dot(r.w_out[...], grad_low).astype(BF16).astype(F32)
            stream.wait(*copies[1])
            norm_again(i)
            for copy in copies[2:]:
                stream.wait(*copy)

            @pl.when(i + 1 < items)
            def _():
                for copy in item_copies(i + 1):
                    stream.start(*copy)
            views = []
            for k in range(pair):
                here, number = pl.ds(k * length, length), i * pair + k
                cols, group = block_at(number, length), pl.ds(k * HEADS, HEADS)
                views.append((r.project.at[i % 2, :, here], r.scaled.at[:, here], r.powers.at[i % 2, k], r.scores.at[group], r.grads.at[group], cols))
                heads.scale_grad(r.grad_mixed.at[:, here], r.inv.at[number], r.mixed.at[:, cols], r.scaled.at[:, here], r.lean.at[number])
            for project, scaled, powers, scores, grads, cols in views:
                heads.grad_probs(project, scaled, scores)
            for k, (project, scaled, powers, scores, grads, cols) in enumerate(views):
                heads.grad_scores(powers, scores, r.lean.at[i * pair + k], grads)
                heads.grad_project(project, scaled, powers, grads, r.gp_f, cols)

        if nz:
            greet(nz)
        fetch(0)
        first_copies = item_copies(0)
        stream.start(*first_copies[0])
        fetch(1)
        for copy in first_copies[1:]:
            stream.start(*copy)
        r.ln1[...] = jnp.zeros_like(r.ln1)
        r.d_char[...] = jnp.zeros_like(r.d_char)
        fetched(0, 1)

        def items_loop(i, _):
            item(i)
            if nz:
                at_step(i, [[lambda: fetch(6), lambda: greeted(nz), down.cores], [lambda: fetched(6), down.corners]])
            return 0
        lax.fori_loop(0, items, items_loop, 0)
        fetch(2, 3, 4, 5)
        for m in range(2):
            stream.start(*act_copy(m))
        if nz:
            down.sides()
        products()
        fetched(2)

        def back_loop(i, _):
            layer_back(i)
            if nz:
                at_step(i, [[ats[3].corners], [ats[0].sides, ats[1].sides, down.lines], [ats[2].sides, ats[3].sides], [ats[0].lines, ats[1].lines]])
            return 0
        lax.fori_loop(0, items, back_loop, 0)
        fetched(3)
        rest_products()
        fetched(4, 5)
        if nz:
            rest.cores()
            ats[2].lines()
            ats[3].lines()

        def result_loop(m, _):
            result(m)
            if nz:
                at_step(m, [[rest.corners]] + [[]] * (chunks - 3) + [[rest.sides]])
            return 0
        lax.fori_loop(0, chunks, result_loop, 0)
        if nz:
            r.o_down[...] = down.total()
            r.o_out[...] = ats[0].total()
            for p in range(3):
                r.o_qkv[:, p * feat:(p + 1) * feat] = ats[1 + p].total()
            rest.lines()
            total = rest.total()
            r.o_time[...] = total[:, 128:]
            r.o_char[...] = total[:, :chars]
            r.o_ln[...] = total[:, :128].T[chars:chars + 4]
        for i in range(items):
            stream.wait(*d_in_copy(i))
        for m in range(chunks):
            stream.wait(*result_copy(m))

    return call.run(kernel, "backward", None, 1 if nz else None)


def hand_over(result, d_in, ln, *others, width=1024):
    feat, n = d_in.shape
    call = Call()
    turned = ((n, feat), F32, pl.BlockSpec((width, feat), lambda i: (i, 0)))
    call.arg(result=(result, lanes(feat, width)), d_in=(d_in, lanes(feat, width)), ln=(ln, whole(ln.shape)))
    call.arg(**{f"a{k}": (value, whole(value.shape)) for k, value in enumerate(others)})
    call.out(o_result=turned, o_d_in=turned, **{f"l{k}": ((1, ln.shape[1]), F32, whole((1, ln.shape[1]))) for k in range(4)})
    call.out(**{f"o{k}": (value.shape, F32, whole(value.shape)) for k, value in enumerate(others)})

    def kernel(r):
        r.o_result[...] = r.result[...].T
        r.o_d_in[...] = r.d_in[...].T

        @pl.when(pl.program_id(0) == 0)
        def _():
            for k, ref in enumerate((r.l0, r.l1, r.l2, r.l3)):
                ref[...] = r.ln[k:k + 1]
            for k in range(len(others)):
                getattr(r, f"o{k}")[...] = getattr(r, f"a{k}")[...]

    got = call.run(kernel, "hand_over", n // width)
    return got.o_result, got.o_d_in, [getattr(got, f"l{k}") for k in range(4)], [getattr(got, f"o{k}") for k in range(len(others))]


def make_body(gx, gy):
    def gathered(*shards):
        return [lax.all_gather(s, AXES, axis=0, tiled=True) for s in shards]

    def summed(part):
        return lax.psum_scatter(part.astype(F32), AXES, scatter_dimension=0, tiled=True)

    def body(tokens, timesteps, cotangent, char_table, time_weight, ln1_gain, ln1_bias, w_qkv, w_attn_out, ln2_gain, ln2_bias, w_up, w_down):
        feat = time_weight.shape[1]
        chars = char_table.shape[0]
        per = feat // (gx * gy)
        nz = gx // 2 if gy == 4 and gx % 8 == 0 and per % 16 == 0 else 0
        shards = [char_table.T, ln1_gain, ln1_bias, ln2_gain, ln2_bias, time_weight, w_qkv, w_attn_out, w_up, w_down]
        if not nz:
            shards = gathered(*shards)
        saved = forward(nz, tokens, timesteps, cotangent, *shards)
        if nz:
            small, w_qkv, w_out = (value.reshape(feat, value.shape[-1]) for value in (saved.first_o, saved.qkv_o, saved.out_o))
            got = backward(nz, chars, tokens, small, w_qkv, w_out, saved)
            ln, sums = got.o_ln, (got.o_char, got.o_time, got.o_qkv, got.o_out, saved.o_up, got.o_down)
        else:
            got = backward(nz, chars, tokens, saved.small, *shards[6:8], saved)
            up, down, at, rest = (summed(p) for p in (saved.d_up, saved.d_down_o, got.d_at, got.d_rest))
            ln, sums = rest[:, chars:chars + 4].T, (rest[:, :chars], rest[:, 128:], at[:, feat:], at[:, :feat], up, down)
        result, d_in, lns, (char, time, qkv, out, up, down) = hand_over(got.result, got.d_in, ln, *sums)
        g1, b1, g2, b2 = (value.reshape(per) for value in lns)
        return result, d_in, char.T, time, g1, b1, qkv, out, g2, b2, up, down
    return body


def solution(mesh):
    every = P(AXES)
    rows, cols = P(AXES, None), P(None, AXES)
    return jax.shard_map(
        make_body(mesh.shape[AXES[0]], mesh.shape[AXES[1]]),
        mesh=mesh,
        in_specs=(every, every, rows, cols, rows, every, every, rows, rows, every, every, rows, rows),
        out_specs=(rows, rows, cols, rows, every, every, rows, rows, every, every, rows, rows),
        check_vma=False,
    )
```

profile of v0, /device:TPU:0, one launch (start us, length us, event | category | flops | bytes accessed | tf_op | source)
XLA Modules:
  0.0 134.0 jit_solution(7871281402136717875)
XLA Ops:
  0.6 79.4 %forward_and_ffn.1 = (f32[512,2048]{1,0:T(8,128)}, bf16[512,2048]{1,0:T(8,128)(2,1)}, bf16[1536,2048]{1,0:T(8,128)(2,1)}, bf16[8,8,256,256]{3,2,1,0:T(8,128)(2,1...) custom-call(s32[8,1,256]{2,1,0:T(1,128)} %bitcast.20, ...), custom_call_target="tpu_custom_call" | custom-call | tf_op jit(solution)/shard_map/forward_and_ffn/pallas_call | solution.py:233
  80.1 46.8 %backward.1 = (f32[512,2048]{1,0:T(8,128)}, f32[512,2048]{1,0:T(8,128)}, f32[16,512]{1,0:T(8,128)}, f32[64,512]{1,0:T(8,128)}, f32[16,1536]{1,0:T(8,128)}, /*ind...) custom-call(s32[8,1,256]{2,1,0:T(1,128)} %bitcast.21, bf16[512,128]{1,0:T(8,128)(2,1)} %get-tuple-element.48.refs_1_, ...), custom_call_target="tpu_custom_call" | custom-call | tf_op jit(solution)/shard_map/backward/pallas_call | solution.py:233
  126.9 7.0 %hand_over.1 = (f32[2048,512]{1,0:T(8,128)}, f32[2048,512]{1,0:T(8,128)}, f32[1,16]{1,0:T(1,128)}, f32[1,16]{1,0:T(1,128)}, f32[1,16]{1,0:T(1,128)}, /*index=5*/...) custom-call(f32[512,2048]{1,0:T(8,128)} %get-tuple-element.63.refs_0, ...), custom_call_target="tpu_custom_call" | custom-call | tf_op jit(solution)/shard_map/hand_over/pallas_call | solution.py:233
where the time goes:
time: 134 us
  Pallas kernels  133 us (99%)
    pallas_call x3, Pallas kernels, run(): pl.pallas_call(body, grid=() if steps is None else (steps,), in_specs=[sp...  133 us

commit v1 on v0

--- a/solution.py
+++ b/solution.py
@@ -411,7 +411,7 @@
              powers_o=((seqs, HEADS, length, length), BF16, ANYWHERE), inv=((seqs, HEADS, length), F32, RESIDENT),
              waves=((feat, 128), BF16, RESIDENT), grad_o=((feat, n), F32, ANYWHERE), ln=((2, feat, 128), F32, RESIDENT),
              d_down_o=((ff, feat), BF16, ANYWHERE), middle_o=((feat, n), F32, ANYWHERE), act_o=((ff, n), BF16, ANYWHERE),
-             down_o=((feat, ff), BF16, ANYWHERE))
+             down_o=((feat, ff), BF16, ANYWHERE), d_out_o=((feat, feat), BF16, ANYWHERE))
     parts = 3
     vmem = lambda kind, *shape: pltpu.VMEM(shape, kind)
     if nz:
@@ -431,9 +431,9 @@
               table=vmem(BF16, feat, 128), out_t=vmem(BF16, feat, feat), starts=vmem(F32, feat, n), mixed=vmem(BF16, feat, n),
               powers=vmem(BF16, 2, pair, HEADS, length, length), scores=vmem(F32, pair * HEADS, length, length),
               middle=vmem(F32, feat, n), low2=vmem(BF16, feat, n), cot_t=vmem(BF16, max(n, ff), feat), cot_f=vmem(BF16, feat, n),
-              down_t=vmem(BF16, feat, ff), up=vmem(BF16, feat, ff), up_t=vmem(BF16, wide, feat),
+              d_out=vmem(BF16, feat, feat), down_t=vmem(BF16, feat, ff), up=vmem(BF16, feat, ff), up_t=vmem(BF16, wide, feat),
               act=vmem(BF16, ff, n), gh=vmem(BF16, ff, n), gn=vmem(F32, feat, chunk), tile_down=vmem(BF16, wide, feat),
-              sems=pltpu.SemaphoreType.DMA((14 + 2 * chunks,)))
+              sems=pltpu.SemaphoreType.DMA((15 + 2 * chunks,)))
 
     def kernel(r):
         proj, low = r.act.at[pl.ds(0, 3 * feat)], r.gh.at[pl.ds(0, feat)]
@@ -476,6 +476,7 @@
             proj[p * feat:(p + 1) * feat] = dot(weights.T, low[...]).astype(BF16)
 
         to_hbm = [(proj, r.project_o), (r.starts, r.start_o), (r.mixed, r.mixed_o), (r.middle, r.middle_o), (r.act, r.act_o), (r.down_t, r.down_o)]
+        d_out_copy = (14 + 2 * chunks, r.d_out, r.d_out_o)
         if nz:
             every = (pl.ds(0, nz), slice(None), slice(None), slice(None), slice(None))
             to_hbm += [(r.first, r.first_o), (r.out, r.out_o)] + [(g.out, r.qkv_o.at[every + (pl.ds(p * feat, feat),)]) for p, g in enumerate(qkv)]
@@ -539,33 +540,36 @@
             down.lines()
             first.cores()
             k.corners()
+            v.corners()
             out.sides()
             first.whole()
             stamps(flat(r.first, slice(128, 128 + feat)))
             begin(range(0, seqs // 2))
             q.cores()
-            v.corners()
             ups[0].sides()
             begin(range(seqs // 2, seqs))
             k.cores()
-            out.corners()
             q.whole()
             multiply(0, flat(r.qkv[0]))
             v.cores()
+            out.corners()
             ups[1].sides()
             for g in ups[2:]:
                 g.lines()
             k.whole()
             multiply(1, flat(r.qkv[1]))
-            out.cores()
             down.arrived()
             needs[0][1].sides()
             v.whole()
             multiply(2, flat(r.qkv[2]))
             ups[0].corners()
+            leave(0, 1)
+
+        def out_weights():
+            out.cores()
             out.whole()
             r.out_t[...] = flat(r.out).T
-            leave(0, 1, *range(6, 8 + parts))
+            leave(*range(6, 8 + parts))
 
         def item(i):
             views = []
@@ -578,6 +582,8 @@
                 heads.softmax(scores, powers, inverses)
                 heads.mix(project, powers, inverses, mixed)
             stream.start(*powers_copy(i))
+            if nz:
+                at_step(i, [[out_weights]])
             cols = block_at(i, width)
             table = small()
             middle = r.starts[:, cols] + dot(r.out_t[...], r.mixed[:, cols])
@@ -589,14 +595,24 @@
         def weights_step(step):
             if not nz:
                 return []
-            acts = [part.cores for part in order[max(2 * step - 2, 0):2 * step]]
-            acts += [part.corners for part in order[max(2 * step, 1):2 * step + 2]]
-            return acts + [part.sides for part in order[2 * step + 4 if step else 3:2 * step + 6]]
+            cores = lambda p: p + 1 if p < 4 else p // 2 + 3
+            corners = lambda p: p - 1 if p < 3 else (p + 1) // 2
+            acts = [part.cores for p, part in enumerate(order) if cores(p) == step]
+            acts += [part.corners for p, part in enumerate(order) if p > 0 and corners(p) == step]
+            return acts + [part.sides for part in order[2 * step + 3:2 * step + 5]]
 
         def sums_step(step):
             if not nz:
                 return []
-            return [(g.corners, g.sides, g.lines)[step - j - 1] for j, g in enumerate(groups) if 0 <= step - j - 1 < 3]
+            late = tiles - 3
+            acts = []
+            for j in reversed(range(tiles)):
+                stage = step - j - 1
+                if j == late and step in (tiles, tiles + 1):
+                    stage = 2 if step == tiles + 1 else -1
+                if 0 <= stage < 3:
+                    acts.append((groups[j].corners, groups[j].sides, groups[j].lines)[stage])
+            return acts
 
         def tile(j):
             rows = block_at(j, wide)
@@ -627,11 +643,14 @@
         def layer_back(m):
             cols, rows = block_at(m, chunk), block_at(m, share)
             r.gn[...] = dot(r.up[...], r.gh[:, cols])
+            at_step(m, [sums_step(tiles + k) for k in range(chunks)])
             r.cot_t[rows, :] = dot_nt(r.act[rows, :], r.cot_f[...]).astype(BF16)
             stream.start(*d_down_copy(m))
             normed, inverse = norm_rows(r.middle[:, cols])
             grad_normed = r.gn[...]
-            r.starts[:, cols] = r.cot_f[:, cols].astype(F32) + norm_rows_back(grad_normed, param(small(), chars + 2), normed, inverse)
+            grad = r.cot_f[:, cols].astype(F32) + norm_rows_back(grad_normed, param(small(), chars + 2), normed, inverse)
+            r.starts[:, cols] = grad
+            r.low2[:, cols] = grad.astype(BF16)
             r.ln[0] += fold(grad_normed * normed)
             r.ln[1] += fold(grad_normed)
             stream.start(*grad_copy(m))
@@ -658,15 +677,17 @@
 
         def chunks_loop(m, _):
             layer_back(m)
-            at_step(m, [sums_step(tiles + k) for k in range(chunks)])
             return 0
         lax.fori_loop(0, chunks, chunks_loop, 0)
+        r.d_out[...] = dot_nt(r.mixed[...], r.low2[...]).astype(BF16)
+        stream.start(*d_out_copy)
         if nz:
             for g in (first, *qkv, out, *ups, down):
                 g.finish()
             for j in range(tiles):
                 r.o_up[:, j * wide:(j + 1) * wide] = groups[j].total()
         left(*range(2, len(to_hbm)))
+        stream.wait(*d_out_copy)
         for i in range(max(items - 2, 0), items):
             stream.wait(*powers_copy(i))
         for m in range(chunks):
@@ -696,7 +717,7 @@
               grad=vmem(F32, feat, n), project=vmem(BF16, 2, 3 * feat, width), powers=vmem(BF16, 2, pair, HEADS, length, length),
               mixed=vmem(BF16, feat, n), ln2=vmem(F32, 2, feat, 128), middle=vmem(F32, feat, n), act=vmem(BF16, 2, ff, chunk),
               down_t=vmem(BF16, feat, ff), ln1=vmem(F32, 2, feat, 128), d_char=vmem(F32, feat, 128), low_f=vmem(BF16, feat, n),
-              gp_f=vmem(BF16, 3 * feat, n), ga_f=vmem(BF16, feat, n), scores=vmem(F32, pair * HEADS, length, length),
+              gp_f=vmem(BF16, 3 * feat, n), scores=vmem(F32, pair * HEADS, length, length),
               grads=vmem(BF16, pair * HEADS, length, length), grad_mixed=vmem(F32, feat, width), scaled=vmem(BF16, feat, width),
               lean=vmem(F32, seqs, HEADS, length), gn=vmem(F32, feat, width), sems=pltpu.SemaphoreType.DMA((12 + 4 * items + chunks,)))
     parts = 4
@@ -704,7 +725,7 @@
         devices = nz * 8
         per, down_per = feat // devices, ff // devices
         blocks = (nz,) + BLOCKS
-        call.arg(d_down=there(saved.d_down_o.reshape(blocks + (down_per, feat))))
+        call.arg(d_down=there(saved.d_down_o.reshape(blocks + (down_per, feat))), d_out_i=there(saved.d_out_o.reshape(blocks + (per, feat))))
         small_out = lambda *shape: (shape, F32, RESIDENT)
         call.out(o_out=small_out(per, feat), o_down=small_out(down_per, feat), o_qkv=small_out(per, 3 * feat), o_time=small_out(per, feat),
                  o_char=small_out(per, chars), o_ln=small_out(4, per))
@@ -712,14 +733,14 @@
                   at_sums=Scatter.scratch(nz, (per, feat)) * parts, kept=vmem(BF16, nz, 2, 2, down_per, feat),
                   d_at=[vmem(BF16, *blocks, per, feat)] * parts, d_rest=vmem(BF16, *blocks, per, 128 + feat))
     else:
-        call.out(d_at=((feat, 4 * feat), BF16, RESIDENT), d_rest=((feat, 128 + feat), BF16, RESIDENT))
+        call.out(d_at=((feat, 3 * feat), BF16, RESIDENT), d_rest=((feat, 128 + feat), BF16, RESIDENT))
 
     def kernel(r):
         stream = Stream(r.sems)
         if nz:
             c = place()[3]
             down = Scatter(nz, r.d_down, r.down_sums, r.kept)
-            ats = [Scatter(nz, r.d_at[p], r.at_sums[5 * p:5 * p + 5]) for p in range(parts)]
+            *ats, out = [Scatter(nz, r.d_at[p], r.at_sums[5 * p:5 * p + 5]) for p in range(parts)]
             rest = Scatter(nz, r.d_rest, r.rest_sums)
 
         def tall(value):
@@ -732,7 +753,7 @@
         fixed = [(r.out_i, r.w_out), (r.small_i.at[:, pl.ds(0, 128)], r.small), (r.qkv_i, r.qkv), (r.ln2_i, r.ln2), (r.middle_i, r.middle),
                  (r.down_i, r.down_t)]
         if nz:
-            fixed.append((r.d_down.at[pl.ds(0, nz), :, :, c], r.kept))
+            fixed += [(r.d_down.at[pl.ds(0, nz), :, :, c], r.kept), (r.d_out_i, r.d_at[3])]
 
         def fetch(*numbers):
             for k in numbers:
@@ -762,17 +783,13 @@
             normed, _ = norm_rows(r.start[:, columns(i)])
             r.low_f[:, columns(i)] = (normed * param(r.small[...], chars) + param(r.small[...], chars + 1)).astype(BF16)
 
-        def products():
-            pairs = [(r.mixed, r.ga_f)] + [(r.low_f, r.gp_f.at[pl.ds(p * feat, feat)]) for p in range(3)]
-            for p, (left, right) in enumerate(pairs):
-                product = tall(dot_nt(left[...], right[...]))
-                if nz:
-                    r.d_at[p][...] = product
-                    ats[p].cores()
-                    if p > 0:
-                        ats[p - 1].corners()
-                else:
-                    r.d_at[:, p * feat:(p + 1) * feat] = product
+        def product(p):
+            value = tall(dot_nt(r.low_f[...], r.gp_f[p * feat:(p + 1) * feat, :]))
+            if nz:
+                r.d_at[p][...] = value
+                ats[p].cores()
+            else:
+                r.d_at[:, p * feat:(p + 1) * feat] = value
 
         def layer_back(i):
             r.gn[...] = dot(r.qkv[...], r.gp_f[:, columns(i)])
@@ -813,12 +830,13 @@
             copies = item_copies(i)
             stream.wait(*copies[0])
             grad_low = r.grad[:, columns(i)].astype(BF16)
-            r.ga_f[:, columns(i)] = grad_low
             r.grad_mixed[...] = dot(r.w_out[...], grad_low).astype(BF16).astype(F32)
             stream.wait(*copies[1])
             norm_again(i)
             for copy in copies[2:]:
                 stream.wait(*copy)
+            if nz:
+                at_step(i, [[lambda: fetch(6, 7), lambda: greeted(nz), down.cores]])
 
             @pl.when(i + 1 < items)
             def _():
@@ -851,21 +869,22 @@
         def items_loop(i, _):
             item(i)
             if nz:
-                at_step(i, [[lambda: fetch(6), lambda: greeted(nz), down.cores], [lambda: fetched(6), down.corners]])
+                at_step(i, [[lambda: fetched(6, 7), down.corners, out.cores], [out.corners], [down.sides, out.sides]])
             return 0
         lax.fori_loop(0, items, items_loop, 0)
         fetch(2, 3, 4, 5)
         for m in range(2):
             stream.start(*act_copy(m))
-        if nz:
-            down.sides()
-        products()
+        product(0)
+        product(1)
+        if nz:
+            ats[0].corners()
         fetched(2)
 
         def back_loop(i, _):
             layer_back(i)
             if nz:
-                at_step(i, [[ats[3].corners], [ats[0].sides, ats[1].sides, down.lines], [ats[2].sides, ats[3].sides], [ats[0].lines, ats[1].lines]])
+                at_step(i, [[ats[1].corners, down.lines], [ats[0].sides, out.lines], [ats[1].sides], [ats[0].lines]])
             return 0
         lax.fori_loop(0, items, back_loop, 0)
         fetched(3)
@@ -873,25 +892,28 @@
         fetched(4, 5)
         if nz:
             rest.cores()
-            ats[2].lines()
-            ats[3].lines()
+        product(2)
+        if nz:
+            rest.corners()
+            ats[1].lines()
 
         def result_loop(m, _):
             result(m)
             if nz:
-                at_step(m, [[rest.corners]] + [[]] * (chunks - 3) + [[rest.sides]])
+                at_step(m, [[ats[2].corners]] + [[]] * (chunks - 4) + [[rest.sides], [ats[2].sides], [rest.lines]])
             return 0
         lax.fori_loop(0, chunks, result_loop, 0)
         if nz:
             r.o_down[...] = down.total()
-            r.o_out[...] = ats[0].total()
-            for p in range(3):
-                r.o_qkv[:, p * feat:(p + 1) * feat] = ats[1 + p].total()
-            rest.lines()
+            r.o_out[...] = out.total()
+            for p in range(2):
+                r.o_qkv[:, p * feat:(p + 1) * feat] = ats[p].total()
+            ats[2].lines()
             total = rest.total()
             r.o_time[...] = total[:, 128:]
             r.o_char[...] = total[:, :chars]
             r.o_ln[...] = total[:, :128].T[chars:chars + 4]
+            r.o_qkv[:, 2 * feat:] = ats[2].total()
         for i in range(items):
             stream.wait(*d_in_copy(i))
         for m in range(chunks):
@@ -947,7 +969,7 @@
         else:
             got = backward(nz, chars, tokens, saved.small, *shards[6:8], saved)
             up, down, at, rest = (summed(p) for p in (saved.d_up, saved.d_down_o, got.d_at, got.d_rest))
-            ln, sums = rest[:, chars:chars + 4].T, (rest[:, :chars], rest[:, 128:], at[:, feat:], at[:, :feat], up, down)
+            ln, sums = rest[:, chars:chars + 4].T, (rest[:, :chars], rest[:, 128:], at, summed(saved.d_out_o), up, down)
         result, d_in, lns, (char, time, qkv, out, up, down) = hand_over(got.result, got.d_in, ln, *sums)
         g1, b1, g2, b2 = (value.reshape(per) for value in lns)
         return result, d_in, char.T, time, g1, b1, qkv, out, g2, b2, up, down

time: 134 us -> 130 us (0.970)
  Pallas kernels: 133 us -> 129 us
    pallas_call x3, Pallas kernels: 133 us -> 129 us  [run(): pl.pallas_call(body, grid=() if steps is None else (steps,), in_specs=[sp...]
where the time goes in v1:
time: 130 us
  Pallas kernels  129 us (99%)
    pallas_call x3, Pallas kernels, run(): pl.pallas_call(body, grid=() if steps is None else (steps,), in_specs=[sp...  129 us

profile of v1, /device:TPU:0, one launch (start us, length us, event | category | flops | bytes accessed | tf_op | source)
XLA Modules:
  0.0 130.0 jit_solution(9785772592747784960)
XLA Ops:
  0.6 79.6 %forward_and_ffn.1 = (f32[512,2048]{1,0:T(8,128)}, bf16[512,2048]{1,0:T(8,128)(2,1)}, bf16[1536,2048]{1,0:T(8,128)(2,1)}, bf16[8,8,256,256]{3,2,1,0:T(8,128)(2,1...) custom-call(s32[8,1,256]{2,1,0:T(1,128)} %bitcast.22, ...), custom_call_target="tpu_custom_call" | custom-call | tf_op jit(solution)/shard_map/forward_and_ffn/pallas_call | solution.py:233
  80.2 42.6 %backward.1 = (f32[512,2048]{1,0:T(8,128)}, f32[512,2048]{1,0:T(8,128)}, f32[16,512]{1,0:T(8,128)}, f32[64,512]{1,0:T(8,128)}, f32[16,1536]{1,0:T(8,128)}, /*ind...) custom-call(s32[8,1,256]{2,1,0:T(1,128)} %bitcast.23, bf16[512,128]{1,0:T(8,128)(2,1)} %get-tuple-element.49.refs_1_, ...), custom_call_target="tpu_custom_call" | custom-call | tf_op jit(solution)/shard_map/backward/pallas_call | solution.py:233
  122.9 6.9 %hand_over.1 = (f32[2048,512]{1,0:T(8,128)}, f32[2048,512]{1,0:T(8,128)}, f32[1,16]{1,0:T(1,128)}, f32[1,16]{1,0:T(1,128)}, f32[1,16]{1,0:T(1,128)}, /*index=5*/...) custom-call(f32[512,2048]{1,0:T(8,128)} %get-tuple-element.65.refs_0, ...), custom_call_target="tpu_custom_call" | custom-call | tf_op jit(solution)/shard_map/hand_over/pallas_call | solution.py:233

commit v2 on v1

--- a/solution.py
+++ b/solution.py
@@ -260,7 +260,7 @@
 
 
 def block_at(i, width):
-    return pl.ds(pl.multiple_of(i * width, width), width)
+    return pl.ds(i * width if isinstance(i, int) else pl.multiple_of(i * width, width), width)
 
 
 def dot(left, right):
@@ -514,6 +514,8 @@
                 for p in range(parts):
                     multiply(p, r.w_qkv[:, p * feat:(p + 1) * feat])
                 leave(0, 1)
+                stream.wait(*cot_in)
+                r.cot_f[...] = r.cot_t[:n].T
                 return
             greet(nz)
             fill_small(r, chars)
@@ -522,6 +524,8 @@
             r.first_shard[:, 128:] = r.time_w[...]
             for g in (first, out, q, k, v, *ups, down):
                 g.out[z, x, y, c] = g.shard[...]
+            stream.wait(*cot_in)
+            r.cot_f[...] = r.cot_t[:n].T
             greeted(nz)
             first.lines()
             q.lines()
@@ -533,17 +537,17 @@
             out.lines()
             k.sides()
             ups[0].lines()
+            v.sides()
             first.corners()
-            v.sides()
             ups[1].lines()
             q.corners()
             down.lines()
+            k.corners()
             first.cores()
-            k.corners()
+            first.whole()
+            stamps(flat(r.first, slice(128, 128 + feat)))
             v.corners()
             out.sides()
-            first.whole()
-            stamps(flat(r.first, slice(128, 128 + feat)))
             begin(range(0, seqs // 2))
             q.cores()
             ups[0].sides()
@@ -563,10 +567,10 @@
             v.whole()
             multiply(2, flat(r.qkv[2]))
             ups[0].corners()
+            out.cores()
             leave(0, 1)
 
         def out_weights():
-            out.cores()
             out.whole()
             r.out_t[...] = flat(r.out).T
             leave(*range(6, 8 + parts))
@@ -590,13 +594,12 @@
             r.middle[:, cols] = middle
             normed, _ = norm_rows(middle)
             r.low2[:, cols] = (normed * param(table, chars + 2) + param(table, chars + 3)).astype(BF16)
-            r.cot_f[:, cols] = r.cot_t[cols, :].T
 
         def weights_step(step):
             if not nz:
                 return []
-            cores = lambda p: p + 1 if p < 4 else p // 2 + 3
-            corners = lambda p: p - 1 if p < 3 else (p + 1) // 2
+            cores = lambda p: (1, 2, 2, 4)[p] if p < 4 else p // 2 + 3
+            corners = lambda p: 0 if p < 3 else 3 if p < 5 else p // 4 + 3
             acts = [part.cores for p, part in enumerate(order) if cores(p) == step]
             acts += [part.corners for p, part in enumerate(order) if p > 0 and corners(p) == step]
             return acts + [part.sides for part in order[2 * step + 3:2 * step + 5]]
@@ -604,15 +607,12 @@
         def sums_step(step):
             if not nz:
                 return []
-            late = tiles - 3
-            acts = []
-            for j in reversed(range(tiles)):
-                stage = step - j - 1
-                if j == late and step in (tiles, tiles + 1):
-                    stage = 2 if step == tiles + 1 else -1
-                if 0 <= stage < 3:
-                    acts.append((groups[j].corners, groups[j].sides, groups[j].lines)[stage])
-            return acts
+            return [(g.corners, g.sides, g.lines)[step - j - 1] for j, g in enumerate(groups) if 0 <= step - j - 1 < 3]
+
+        middles, ends = [], []
+        if nz:
+            middles = [[groups[-1].corners], [groups[-1].sides, groups[-3].lines]]
+            ends = [[groups[-2].sides], [groups[-2].lines], [groups[-1].lines]]
 
         def tile(j):
             rows = block_at(j, wide)
@@ -643,7 +643,7 @@
         def layer_back(m):
             cols, rows = block_at(m, chunk), block_at(m, share)
             r.gn[...] = dot(r.up[...], r.gh[:, cols])
-            at_step(m, [sums_step(tiles + k) for k in range(chunks)])
+            at_step(m, middles)
             r.cot_t[rows, :] = dot_nt(r.act[rows, :], r.cot_f[...]).astype(BF16)
             stream.start(*d_down_copy(m))
             normed, inverse = norm_rows(r.middle[:, cols])
@@ -656,7 +656,6 @@
             stream.start(*grad_copy(m))
 
         prelude()
-        stream.wait(*cot_in)
 
         def items_loop(i, _):
             @pl.when(i >= 2)
@@ -677,6 +676,7 @@
 
         def chunks_loop(m, _):
             layer_back(m)
+            at_step(m, ends)
             return 0
         lax.fori_loop(0, chunks, chunks_loop, 0)
         r.d_out[...] = dot_nt(r.mixed[...], r.low2[...]).astype(BF16)

time: 130 us -> 128 us (0.985)
  Pallas kernels: 129 us -> 127 us
    pallas_call x3, Pallas kernels: 129 us -> 127 us  [run(): pl.pallas_call(body, grid=() if steps is None else (steps,), in_specs=[sp...]
where the time goes in v2:
time: 128 us
  Pallas kernels  127 us (99%)
    pallas_call x3, Pallas kernels, run(): pl.pallas_call(body, grid=() if steps is None else (steps,), in_specs=[sp...  127 us

profile of v2, /device:TPU:0, one launch (start us, length us, event | category | flops | bytes accessed | tf_op | source)
XLA Modules:
  0.0 127.6 jit_solution(13296066251439528740)
XLA Ops:
  0.6 77.5 %forward_and_ffn.1 = (f32[512,2048]{1,0:T(8,128)}, bf16[512,2048]{1,0:T(8,128)(2,1)}, bf16[1536,2048]{1,0:T(8,128)(2,1)}, bf16[8,8,256,256]{3,2,1,0:T(8,128)(2,1...) custom-call(s32[8,1,256]{2,1,0:T(1,128)} %bitcast.22, ...), custom_call_target="tpu_custom_call" | custom-call | tf_op jit(solution)/shard_map/forward_and_ffn/pallas_call | solution.py:233
  78.2 42.3 %backward.1 = (f32[512,2048]{1,0:T(8,128)}, f32[512,2048]{1,0:T(8,128)}, f32[16,512]{1,0:T(8,128)}, f32[64,512]{1,0:T(8,128)}, f32[16,1536]{1,0:T(8,128)}, /*ind...) custom-call(s32[8,1,256]{2,1,0:T(1,128)} %bitcast.23, bf16[512,128]{1,0:T(8,128)(2,1)} %get-tuple-element.49.refs_1_, ...), custom_call_target="tpu_custom_call" | custom-call | tf_op jit(solution)/shard_map/backward/pallas_call | solution.py:233
  120.5 6.9 %hand_over.1 = (f32[2048,512]{1,0:T(8,128)}, f32[2048,512]{1,0:T(8,128)}, f32[1,16]{1,0:T(1,128)}, f32[1,16]{1,0:T(1,128)}, f32[1,16]{1,0:T(1,128)}, /*index=5*/...) custom-call(f32[512,2048]{1,0:T(8,128)} %get-tuple-element.65.refs_0, ...), custom_call_target="tpu_custom_call" | custom-call | tf_op jit(solution)/shard_map/hand_over/pallas_call | solution.py:233

commit v3 on v2

--- a/solution.py
+++ b/solution.py
@@ -409,7 +409,7 @@
              w_down=at_once(w_down), cot=(cotangent, ANYWHERE))
     call.out(start_o=((feat, n), F32, ANYWHERE), mixed_o=((feat, n), BF16, ANYWHERE), project_o=((3 * feat, n), BF16, ANYWHERE),
              powers_o=((seqs, HEADS, length, length), BF16, ANYWHERE), inv=((seqs, HEADS, length), F32, RESIDENT),
-             waves=((feat, 128), BF16, RESIDENT), grad_o=((feat, n), F32, ANYWHERE), ln=((2, feat, 128), F32, RESIDENT),
+             waves=((feat, 128), BF16, RESIDENT), grad_o=((feat, n), F32, ANYWHERE), ln_o=((2, feat, 128), F32, ANYWHERE),
              d_down_o=((ff, feat), BF16, ANYWHERE), middle_o=((feat, n), F32, ANYWHERE), act_o=((ff, n), BF16, ANYWHERE),
              down_o=((feat, ff), BF16, ANYWHERE), d_out_o=((feat, feat), BF16, ANYWHERE))
     parts = 3
@@ -427,13 +427,13 @@
                  qkv_o=(blocks(*w_qkv.shape), BF16, ANYWHERE), o_up=((per, ff), F32, RESIDENT))
     else:
         call.out(small=((count, 128), BF16, RESIDENT), d_up=((feat, ff), BF16, RESIDENT))
-    call.temp(small_shard=vmem(BF16, count, 128), square=vmem(F32, 128, max(count, 128)), steps_row=vmem(F32, 1, 128),
+    call.temp(ln=vmem(F32, 2, feat, 128), small_shard=vmem(BF16, count, 128), square=vmem(F32, 128, max(count, 128)), steps_row=vmem(F32, 1, 128),
               table=vmem(BF16, feat, 128), out_t=vmem(BF16, feat, feat), starts=vmem(F32, feat, n), mixed=vmem(BF16, feat, n),
               powers=vmem(BF16, 2, pair, HEADS, length, length), scores=vmem(F32, pair * HEADS, length, length),
               middle=vmem(F32, feat, n), low2=vmem(BF16, feat, n), cot_t=vmem(BF16, max(n, ff), feat), cot_f=vmem(BF16, feat, n),
               d_out=vmem(BF16, feat, feat), down_t=vmem(BF16, feat, ff), up=vmem(BF16, feat, ff), up_t=vmem(BF16, wide, feat),
               act=vmem(BF16, ff, n), gh=vmem(BF16, ff, n), gn=vmem(F32, feat, chunk), tile_down=vmem(BF16, wide, feat),
-              sems=pltpu.SemaphoreType.DMA((15 + 2 * chunks,)))
+              sems=pltpu.SemaphoreType.DMA((16 + 2 * chunks,)))
 
     def kernel(r):
         proj, low = r.act.at[pl.ds(0, 3 * feat)], r.gh.at[pl.ds(0, feat)]
@@ -477,6 +477,7 @@
 
         to_hbm = [(proj, r.project_o), (r.starts, r.start_o), (r.mixed, r.mixed_o), (r.middle, r.middle_o), (r.act, r.act_o), (r.down_t, r.down_o)]
         d_out_copy = (14 + 2 * chunks, r.d_out, r.d_out_o)
+        ln_copy = (15 + 2 * chunks, r.ln, r.ln_o)
         if nz:
             every = (pl.ds(0, nz), slice(None), slice(None), slice(None), slice(None))
             to_hbm += [(r.first, r.first_o), (r.out, r.out_o)] + [(g.out, r.qkv_o.at[every + (pl.ds(p * feat, feat),)]) for p, g in enumerate(qkv)]
@@ -679,6 +680,7 @@
             at_step(m, ends)
             return 0
         lax.fori_loop(0, chunks, chunks_loop, 0)
+        stream.start(*ln_copy)
         r.d_out[...] = dot_nt(r.mixed[...], r.low2[...]).astype(BF16)
         stream.start(*d_out_copy)
         if nz:
@@ -688,6 +690,7 @@
                 r.o_up[:, j * wide:(j + 1) * wide] = groups[j].total()
         left(*range(2, len(to_hbm)))
         stream.wait(*d_out_copy)
+        stream.wait(*ln_copy)
         for i in range(max(items - 2, 0), items):
             stream.wait(*powers_copy(i))
         for m in range(chunks):
@@ -710,7 +713,7 @@
     call = Call()
     call.arg(tok=(tokens.reshape(seqs, 1, length), RESIDENT), waves=(saved.waves, RESIDENT), inv=(saved.inv, RESIDENT), small_i=there(small),
              qkv_i=there(w_qkv), out_i=there(w_out), start_i=there(saved.start_o), grad_i=there(saved.grad_o), project_i=there(saved.project_o),
-             powers_i=there(saved.powers_o), mixed_i=there(saved.mixed_o), ln2_i=there(saved.ln),
+             powers_i=there(saved.powers_o), mixed_i=there(saved.mixed_o), ln2_i=there(saved.ln_o),
              middle_i=there(saved.middle_o), act_i=there(saved.act_o), down_i=there(saved.down_o))
     call.out(d_in=((feat, n), F32, ANYWHERE), result=((feat, n), F32, ANYWHERE))
     call.temp(small=vmem(BF16, feat, 128), qkv=vmem(BF16, feat, 3 * feat), w_out=vmem(BF16, feat, feat), start=vmem(F32, feat, n),
@@ -832,6 +835,7 @@
             grad_low = r.grad[:, columns(i)].astype(BF16)
             r.grad_mixed[...] = dot(r.w_out[...], grad_low).astype(BF16).astype(F32)
             stream.wait(*copies[1])
+            at_step(i, [[lambda: fetched(1)]])
             norm_again(i)
             for copy in copies[2:]:
                 stream.wait(*copy)
@@ -864,7 +868,7 @@
             stream.start(*copy)
         r.ln1[...] = jnp.zeros_like(r.ln1)
         r.d_char[...] = jnp.zeros_like(r.d_char)
-        fetched(0, 1)
+        fetched(0)
 
         def items_loop(i, _):
             item(i)

time: 128 us -> 128 us (level)
  no operation moved by 1% of the time
where the time goes in v3:
time: 128 us; the launch traced here: 127 us
  Pallas kernels  127 us (99%)
    pallas_call x3, Pallas kernels, run(): pl.pallas_call(body, grid=() if steps is None else (steps,), in_specs=[sp...  127 us

profile of v3, /device:TPU:0, one launch (start us, length us, event | category | flops | bytes accessed | tf_op | source)
XLA Modules:
  0.0 127.4 jit_solution(10196770571841222346)
XLA Ops:
  0.6 77.3 %forward_and_ffn.1 = (f32[512,2048]{1,0:T(8,128)}, bf16[512,2048]{1,0:T(8,128)(2,1)}, bf16[1536,2048]{1,0:T(8,128)(2,1)}, bf16[8,8,256,256]{3,2,1,0:T(8,128)(2,1...) custom-call(s32[8,1,256]{2,1,0:T(1,128)} %bitcast.22, ...), custom_call_target="tpu_custom_call" | custom-call | tf_op jit(solution)/shard_map/forward_and_ffn/pallas_call | solution.py:233
  78.0 42.3 %backward.1 = (f32[512,2048]{1,0:T(8,128)}, f32[512,2048]{1,0:T(8,128)}, f32[16,512]{1,0:T(8,128)}, f32[64,512]{1,0:T(8,128)}, f32[16,1536]{1,0:T(8,128)}, /*ind...) custom-call(s32[8,1,256]{2,1,0:T(1,128)} %bitcast.23, bf16[512,128]{1,0:T(8,128)(2,1)} %get-tuple-element.49.refs_1_, ...), custom_call_target="tpu_custom_call" | custom-call | tf_op jit(solution)/shard_map/backward/pallas_call | solution.py:233
  120.3 6.9 %hand_over.1 = (f32[2048,512]{1,0:T(8,128)}, f32[2048,512]{1,0:T(8,128)}, f32[1,16]{1,0:T(1,128)}, f32[1,16]{1,0:T(1,128)}, f32[1,16]{1,0:T(1,128)}, /*index=5*/...) custom-call(f32[512,2048]{1,0:T(8,128)} %get-tuple-element.65.refs_0, ...), custom_call_target="tpu_custom_call" | custom-call | tf_op jit(solution)/shard_map/hand_over/pallas_call | solution.py:233
